TPU v7x, 1024 devices: a whole 4x8x16 slice. The times are simulated.
1024 devices in a mesh: dp: 16 (over z), group: 8 (over y), inner: 8 (over x, core).
Axes of the slice: x: 4, y: 8, z: 16, core: 2. Of those that a mesh axis runs over, the one named last changes fastest.
Arguments:
- token_inputs: bfloat16 [1024, 3584], P(('group', 'inner')), may hold values from -1 to 1
- out_grads: bfloat16 [1024, 3584], P(('group', 'inner')), may hold values from -2 to 2
- expert_ids: int32 [1024, 8], P(('group', 'inner')), may hold values from 0 to 127, as said below
- router_weight: float32 [3584, 128], replicated, may hold values from -1.6 to 1.6
- gate_weight: bfloat16 [128, 3584, 1024], P(('group', 'inner'), None, 'dp'), may hold values from -0.09375 to 0.09375
- up_weight: bfloat16 [128, 3584, 1024], P(('group', 'inner'), None, 'dp'), may hold values from -0.09375 to 0.09375
- down_weight: bfloat16 [128, 1024, 3584], P(('group', 'inner'), 'dp'), may hold values from -0.1875 to 0.1875
- saved_gate: bfloat16 [128, 128, 1024], P(('group', 'inner'), None, 'dp'), may hold values from -6 to 6
- saved_up: bfloat16 [128, 128, 1024], P(('group', 'inner'), None, 'dp'), may hold values from -6 to 6
Outputs:
- input_grad: bfloat16 [1024, 3584], P(('group', 'inner'), 'dp')
- router_grad: float32 [3584, 128], P('dp')
Inputs may be any that keep to these rules, and one draw needn't show every extreme that they name: `expert_ids`: each token names 8 different experts, 2 in each of 4 node groups, expert e lying in node group e // 16. One node group is among those of every token. Among the 16 tokens of one block (the rows of one device) no expert is named more than 2 times, and in every block some experts are named exactly 2 times.
All inputs are finite; a program needn't handle non-finite values.
Results may differ from a plain program's by a relative error of at most 0.014.
Values may be sent and summed in bfloat16 or wider, within the bound.
A program may use at most 32 MiB of HBM per device.

v0:
```python
import jax
import jax.numpy as jnp
from jax import lax
from jax.sharding import PartitionSpec as P

route_scale = 2.5


def route_slots(expert_ids, experts_all, capacity):
    matches = (
        expert_ids[:, :, None] == jnp.arange(experts_all, dtype=jnp.int32)[None, None, :]
    ).astype(jnp.int32)
    per_token = jnp.sum(matches, axis=1)
    earlier = jnp.cumsum(per_token, axis=0) - per_token
    position = jnp.sum(matches * earlier[:, None, :], axis=2)
    return (expert_ids * capacity + position, matches)


def router_terms(gate_grads, chosen, affinity_sum, matches):
    weighted = jnp.sum(gate_grads * chosen, axis=1, keepdims=True)
    logit_grads = (
        route_scale
        * (gate_grads / affinity_sum - weighted / (affinity_sum * affinity_sum))
        * chosen
        * (1.0 - chosen)
    )
    return jnp.sum(matches.astype(jnp.float32) * logit_grads[:, :, None], axis=1)


def expert_backward(received, gate_weight, up_weight, down_weight, saved_gate, saved_up):
    experts_here, slot_count, hidden_here = saved_gate.shape
    sources = received.shape[0]
    capacity = slot_count // sources
    hidden_grad = jnp.einsum(
        "sjcd,jfd->jscf", received, down_weight, preferred_element_type=jnp.float32
    )
    pre_gate = saved_gate.reshape(experts_here, sources, capacity, hidden_here).astype(jnp.float32)
    pre_up = saved_up.reshape(experts_here, sources, capacity, hidden_here).astype(jnp.float32)
    sigmoid_gate = jax.nn.sigmoid(pre_gate)
    swish_gate = pre_gate * sigmoid_gate
    gate_part = jnp.sum(swish_gate * pre_up * hidden_grad, axis=3)
    d_gate = (hidden_grad * pre_up * sigmoid_gate * (1.0 + pre_gate * (1.0 - sigmoid_gate))).astype(
        jnp.bfloat16
    )
    d_up = (hidden_grad * swish_gate).astype(jnp.bfloat16)
    both_grads = jnp.concatenate((d_gate, d_up), axis=3)
    both_weights = jnp.concatenate((gate_weight, up_weight), axis=2)
    rows_back = jnp.einsum(
        "jscg,jdg->sjcd", both_grads, both_weights, preferred_element_type=jnp.float32
    )
    return (
        rows_back.astype(jnp.bfloat16),
        jnp.transpose(gate_part, (1, 0, 2)).astype(jnp.bfloat16),
    )


def local(
    token_inputs,
    out_grads,
    expert_ids,
    router_weight,
    gate_weight,
    up_weight,
    down_weight,
    saved_gate,
    saved_up,
):
    group_count = lax.axis_size("group")
    inner_count = lax.axis_size("inner")
    ep_devices = group_count * inner_count
    experts_here = gate_weight.shape[0]
    experts_all = router_weight.shape[1]
    capacity = saved_gate.shape[1] // ep_devices
    model_width = token_inputs.shape[1]
    flat_slot, matches = route_slots(expert_ids, experts_all, capacity)
    placement = jnp.sum(
        (
            flat_slot[:, :, None]
            == jnp.arange(experts_all * capacity, dtype=jnp.int32)[None, None, :]
        ).astype(jnp.bfloat16),
        axis=1,
    )
    outgoing = jnp.einsum(
        "te,td->ed", placement, out_grads, preferred_element_type=jnp.float32
    ).astype(jnp.bfloat16)
    outgoing = outgoing.reshape(ep_devices, experts_here, capacity, model_width)
    received = lax.all_to_all(outgoing, ("group", "inner"), split_axis=0, concat_axis=0, tiled=True)
    rows_back, gate_back = expert_backward(
        received, gate_weight, up_weight, down_weight, saved_gate, saved_up
    )
    rows_home, gate_home = (
        lax.all_to_all(rows_back, ("group", "inner"), split_axis=0, concat_axis=0, tiled=True),
        lax.all_to_all(gate_back, ("group", "inner"), split_axis=0, concat_axis=0, tiled=True),
    )
    rows_home = rows_home.reshape(experts_all * capacity, model_width)
    gate_home = gate_home.reshape(experts_all * capacity)
    scores = jnp.dot(
        token_inputs.astype(jnp.float32), router_weight, precision=lax.Precision.HIGHEST
    )
    affinity = jax.nn.sigmoid(scores)
    chosen = jnp.take_along_axis(affinity, expert_ids, axis=1)
    affinity_sum = jnp.sum(chosen, axis=1, keepdims=True)
    mixing = route_scale * chosen / affinity_sum
    picked = jnp.take(rows_home, flat_slot, axis=0).astype(jnp.float32)
    expert_sum = jnp.sum(mixing[:, :, None] * picked, axis=1)
    gate_partial = jnp.take(gate_home, flat_slot, axis=0).astype(jnp.float32)
    slice_width = model_width // lax.axis_size("dp")
    slice_start = lax.axis_index("dp") * slice_width
    summed = lax.psum_scatter(expert_sum, "dp", scatter_dimension=1, tiled=True)
    gate_total = lax.psum(gate_partial, "dp")
    logit_grads = router_terms(gate_total, chosen, affinity_sum, matches)
    router_slice = lax.dynamic_slice_in_dim(router_weight, slice_start, slice_width, 0)
    summed = summed + jnp.dot(logit_grads, router_slice.T, precision=lax.Precision.HIGHEST)
    columns = lax.dynamic_slice_in_dim(token_inputs, slice_start, slice_width, 1).astype(
        jnp.float32
    )
    router_part = jnp.dot(columns.T, logit_grads, precision=lax.Precision.HIGHEST)
    router_grad = lax.psum(router_part, ("group", "inner"))
    return (summed.astype(jnp.bfloat16), router_grad)


def solution(mesh):
    placed = (
        P(("group", "inner"), None),
        P(("group", "inner"), None),
        P(("group", "inner"), None),
        P(),
        P(("group", "inner"), None, "dp"),
        P(("group", "inner"), None, "dp"),
        P(("group", "inner"), "dp", None),
        P(("group", "inner"), None, "dp"),
        P(("group", "inner"), None, "dp"),
    )
    return jax.shard_map(
        local,
        mesh=mesh,
        in_specs=placed,
        out_specs=(P(("group", "inner"), "dp"), P("dp", None)),
        check_vma=False,
    )
```

profile of v0, /device:TPU:1, one launch (start us, length us, event | category | flops | bytes accessed | tf_op | source)
XLA Modules:
  0.0 379.0 jit_solution(9448215782119511138)
XLA Ops:
  8.0 0.9 copy.85
  8.9 0.1 convert_reduce_fusion
  9.0 0.4 select_reduce_fusion
  9.5 0.1 fusion.15
  9.6 2.8 convolution_convert_fusion.1
  12.4 4.8 %reshape.66 = bf16[64,2,2,3584]{3,2,1,0:T(2,128)(2,1)} reshape(bf16[256,3584]{1,0:T(8,128)(2,1)} %convolution_convert_fusion.1) | data formatting | bytes 3670016 | tf_op jit(solution)/shard_map/reshape | solution.py:86
  17.2 19.2 %all-to-all-start = ((bf16[64,2,2,3584]{3,2,1,0:T(2,128)(2,1)}), bf16[64,2,2,3584]{3,2,1,0:T(2,128)(2,1)}, u32[]{:S(2)}, u32[]{:S(2)}) async-start(bf16[64,2,2,3584]{3,2,1,0:T(2,128)(2,1)} %reshape.66), calls=%async_computation | async-start | bytes 3670016 | tf_op jit(solution)/shard_map/all_to_all | solution.py:87
  36.4 0.1 copy.108
  36.5 0.1 copy.109
  36.6 1.7 copy.92
  38.3 2.6 copy.93
  40.9 39.8 %all-to-all-done = bf16[64,2,2,3584]{3,2,1,0:T(2,128)(2,1)} async-done(((bf16[64,2,2,3584]{3,2,1,0:T(2,128)(2,1)}), bf16[64,2,2,3584]{3,2,1,0:T(2,128)(2,1)}, u32[]{:S(2)}, u32[]{:S(2)}) %all-to-all-start) | async-done | bytes 1835040 | tf_op jit(solution)/shard_map/all_to_all | solution.py:87
  80.7 2.5 multiply_reduce_fusion.1
  83.2 0.7 copy.103
  83.9 6.8 %all-to-all-start.2 = ((bf16[64,2,2]{2,1,0:T(2,128)(2,1)}), bf16[64,2,2]{2,1,0:T(2,128)(2,1)S(1)}, u32[]{:S(2)}, u32[]{:S(2)}) async-start(bf16[64,2,2]{2,1,0:T(2,128)(2,1)} %copy.103), calls=%async_computation.2 | async-start | bytes 65536 | tf_op jit(solution)/shard_map/all_to_all | solution.py:93
  90.7 3.2 fusion
  94.0 3.1 copy.101
  97.1 2.9 all-to-all-done.2
  100.0 7.7 %all-to-all-start.1 = ((bf16[64,2,2,3584]{3,2,1,0:T(2,128)(2,1)}), bf16[64,2,2,3584]{3,2,1,0:T(2,128)(2,1)}, u32[]{:S(2)}, u32[]{:S(2)}) async-start(bf16[64,2,2,3584]{3,2,1,0:T(2,128)(2,1)} %copy.101), calls=%async_computation.1 | async-start | bytes 3670016 | tf_op jit(solution)/shard_map/all_to_all | solution.py:92
  107.7 0.0 reduce-scatter.4.cloned.1.call-start
  107.7 0.1 reshape.73
  107.8 0.1 copy.88
  107.9 0.1 copy.89
  108.0 0.1 reshape.87
  108.1 0.7 fusion.8
  108.8 1.3 gather_fusion.2
  110.1 0.1 reshape.90
  110.2 0.1 reshape.68
  110.3 1.2 gather_fusion.1
  111.5 0.1 reshape.80
  111.7 32.2 %psum.14 = f32[16,8]{1,0:T(8,128)S(1)} all-reduce(f32[16,8]{1,0:T(8,128)S(1)} %get-tuple-element.5), channel_id=1, replica_groups=mesh['dp'=16,'group'=8,'inner'=8] {'dp'}, use_global_device_ids=true, to_apply=%region_8.9 | all-reduce | flops 128 | bytes 1024 | tf_op jit(solution)/shard_map/psum | solution.py:110
  143.8 0.1 multiply_reduce_fusion.2
  144.0 0.1 subtract_multiply_fusion
  144.0 7.8 %all-to-all-done.1 = bf16[64,2,2,3584]{3,2,1,0:T(2,128)(2,1)} async-done(((bf16[64,2,2,3584]{3,2,1,0:T(2,128)(2,1)}), bf16[64,2,2,3584]{3,2,1,0:T(2,128)(2,1)}, u32[]{:S(2)}, u32[]{:S(2)}) %all-to-all-start.1) | async-done | bytes 1835040 | tf_op jit(solution)/shard_map/all_to_all | solution.py:92
  151.9 4.9 %reshape.67 = bf16[256,3584]{1,0:T(8,128)(2,1)} reshape(bf16[64,2,2,3584]{3,2,1,0:T(2,128)(2,1)} %all-to-all-done.1) | data formatting | bytes 3670016 | tf_op jit(solution)/shard_map/reshape | solution.py:95
  156.8 3.8 gather_fusion
  160.6 0.7 multiply_reduce_fusion
  161.3 1.8 copy.106
  163.1 0.0 reduce-scatter.4.cloned.1.call-update
  163.1 0.0 all-reduce.2.cloned.1.call-start
  163.2 0.1 fusion.14
  163.3 1.0 fusion.19
  164.3 0.0 all-reduce.2.cloned.1.call-update
  164.3 61.8 %reduce-scatter.4.cloned.1.call-done = f32[224,16]{1,0:T(8,128)} async-done(((f32[3584,16]{1,0:T(8,128)}), f32[224,16]{1,0:T(8,128)}) %reduce-scatter.4.cloned.1.call-update) | async-done | bytes 14352
  226.1 1.0 copy.107
  227.1 0.9 fusion.5
  228.0 142.0 %all-reduce.2.cloned.1.call-done = f32[224,128]{1,0:T(8,128)} async-done(((f32[224,128]{1,0:T(8,128)}), f32[224,128]{1,0:T(8,128)}) %all-reduce.2.cloned.1.call-update) | async-done | bytes 114704 | tf_op jit(solution)/shard_map/psum | solution.py:118
  370.0 1.6 copy.123
  (17 shorter events, 0.1 us)
Async XLA Ops:
  8.0 100.1 %copy-start = (f32[3584,128]{1,0:T(8,128)S(1)}, f32[3584,128]{1,0:T(8,128)}, u32[]{:S(2)}) copy-start(f32[3584,128]{1,0:T(8,128)} %param.12) | copy-start | bytes 5505028
  17.2 19.2 %copy-start.3 = (bf16[2,128,64]{1,2,0:T(8,128)(2,1)S(1)}, bf16[2,128,64]{1,2,0:T(8,128)(2,1)}, u32[]{:S(2)}) copy-start(bf16[2,128,64]{1,2,0:T(8,128)(2,1)} %param.17) | copy-start | bytes 98308
  17.2 19.3 %copy-start.4 = (bf16[2,128,64]{1,2,0:T(8,128)(2,1)S(1)}, bf16[2,128,64]{1,2,0:T(8,128)(2,1)}, u32[]{:S(2)}) copy-start(bf16[2,128,64]{1,2,0:T(8,128)(2,1)} %param.16) | copy-start | bytes 98308
  17.2 19.4 %copy-start.1 = (bf16[2,3584,64]{1,2,0:T(8,128)(2,1)S(1)}, bf16[2,3584,64]{1,2,0:T(8,128)(2,1)}, u32[]{:S(2)}) copy-start(bf16[2,3584,64]{1,2,0:T(8,128)(2,1)} %param.13) | copy-start | bytes 2752516
  17.2 63.5 %all-to-all-start = ((bf16[64,2,2,3584]{3,2,1,0:T(2,128)(2,1)}), bf16[64,2,2,3584]{3,2,1,0:T(2,128)(2,1)}, u32[]{:S(2)}, u32[]{:S(2)}) async-start(bf16[64,2,2,3584]{3,2,1,0:T(2,128)(2,1)} %reshape.66), calls=%async_computation | async-start | bytes 3670016 | tf_op jit(solution)/shard_map/all_to_all | solution.py:87
  83.9 16.1 %all-to-all-start.2 = ((bf16[64,2,2]{2,1,0:T(2,128)(2,1)}), bf16[64,2,2]{2,1,0:T(2,128)(2,1)S(1)}, u32[]{:S(2)}, u32[]{:S(2)}) async-start(bf16[64,2,2]{2,1,0:T(2,128)(2,1)} %copy.103), calls=%async_computation.2 | async-start | bytes 65536 | tf_op jit(solution)/shard_map/all_to_all | solution.py:93
  97.1 11.0 %copy-start.2 = (bf16[16,3584]{1,0:T(8,128)(2,1)S(1)}, bf16[16,3584]{1,0:T(8,128)(2,1)}, u32[]{:S(2)}) copy-start(bf16[16,3584]{1,0:T(8,128)(2,1)} %param.9) | copy-start | bytes 344068
  100.0 51.9 %all-to-all-start.1 = ((bf16[64,2,2,3584]{3,2,1,0:T(2,128)(2,1)}), bf16[64,2,2,3584]{3,2,1,0:T(2,128)(2,1)}, u32[]{:S(2)}, u32[]{:S(2)}) async-start(bf16[64,2,2,3584]{3,2,1,0:T(2,128)(2,1)} %copy.101), calls=%async_computation.1 | async-start | bytes 3670016 | tf_op jit(solution)/shard_map/all_to_all | solution.py:92
  107.7 118.4 %reduce-scatter.4.cloned.1.call-start = ((), (), s32[]{:S(2)}) async-start(), calls=%async_computation.5 | async-start | bytes 1949696
  163.1 206.9 %all-reduce.2.cloned.1.call-start = ((), (), s32[]{:S(2)}) async-start(), calls=%async_computation.4 | async-start | bytes 229376 | tf_op jit(solution)/shard_map/psum | solution.py:118
Sparse Core Ops, SparseCore 0:
  163.2 62.8 reduce-scatter.3
Sparse Core Ops, SparseCore 1:
  168.0 201.9 all-reduce.1
where the time goes:
time: 380 us; the launch traced here: 379 us
  waiting for transfers between devices  254 us (67%)
  starting transfers between devices  33.7 us (9%)
  blocking collectives  32.2 us (8%)
  local copies, waits for them, and re-layouts  30.1 us (8%)
  between operations  15.7 us (4%)
  matrix products  11.1 us (3%)
    psum x1, waiting for transfers between devices, local(): router_grad = lax.psum(router_part, ('group', 'inner'))  142 us
    unnamed x3, waiting for transfers between devices  61.8 us
    all_to_all x1, waiting for transfers between devices, local(): lax.all_to_all(outgoing, ('group', 'inner'), split_axis=0, concat_axis=0,...  39.8 us
    psum x1, blocking collectives, local(): gate_total = lax.psum(gate_partial, 'dp')  32.2 us
    all_to_all x1, starting transfers between devices, local(): lax.all_to_all(outgoing, ('group', 'inner'), split_axis=0, concat_axis=0,...  19.2 us
    unnamed x18, local copies, waits for them, and re-layouts  9.7 us
    all_to_all x1, waiting for transfers between devices, local(): lax.all_to_all(rows_back, ('group', 'inner'), split_axis=0, concat_axis=0...  7.85 us
    all_to_all x1, starting transfers between devices, local(): lax.all_to_all(rows_back, ('group', 'inner'), split_axis=0, concat_axis=0...  7.66 us
  transfers between devices with their start and end apart: 5, of which 5 were waited for; matrix products, arithmetic and copies ran while one was open for 5% of the time, Pallas kernels for 0%

commit v1 on v0

v1 whole, which is shorter than its diff:
```python
import functools

import jax
import jax.numpy as jnp
from jax import lax
from jax.experimental import pallas as pl
from jax.experimental.pallas import tpu as pltpu
from jax.sharding import PartitionSpec as P

MESH = pl.DeviceIdType.MESH
route_scale = 2.5
f32, bf16 = jnp.float32, jnp.bfloat16
HI = lax.Precision.HIGHEST
CHUNKS = 2


def dot_nt(a, b, **kw):
    return lax.dot_general(a, b, (((1,), (1,)), ((), ())), preferred_element_type=f32, **kw)


def dot_nn(a, b):
    return lax.dot_general(a, b, (((1,), (0,)), ((), ())), preferred_element_type=f32)


def iota(shape, dim):
    return lax.broadcasted_iota(jnp.int32, shape, dim)


def kernel(
    NZ, NG, NI, K,
    pay1, pay2, scores, rw_hbm, gw_hbm, uw_hbm, dw_hbm, sg_hbm, su_hbm,
    out_x, out_r,
    gwv, uwv, dwv, sgv, suv, rwv,
    buf1, buf2, buf3, pt, pmix, wT, tokT, xt, dgu, gz, bufG, gflat, gt, lg,
    rs_src, rs_dst, finv, tbuf, rbuf, ysrc, yacc, ydst,
    load_sem, ys, yr, xs, xr, ag_s, ag_r, rs_s, rs_r, z_s, z_r,
):
    NB = NG * NI
    T = 16 * NB
    S = 2 * NB
    E = 2 * NB
    FP = pay1.shape[1]
    FS = rwv.shape[0]
    F = dwv.shape[1]
    D = dwv.shape[2]
    half = NZ // 2
    CR = FS // CHUNKS
    g, i, n = lax.axis_index("group"), lax.axis_index("inner"), lax.axis_index("dp")
    q = g * NI + i

    loads = [
        pltpu.make_async_copy(dw_hbm, dwv, load_sem.at[0]),
        pltpu.make_async_copy(sg_hbm, sgv, load_sem.at[1]),
        pltpu.make_async_copy(su_hbm, suv, load_sem.at[2]),
        pltpu.make_async_copy(gw_hbm, gwv, load_sem.at[3]),
        pltpu.make_async_copy(uw_hbm, uwv, load_sem.at[4]),
        pltpu.make_async_copy(
            rw_hbm.at[pl.ds(pl.multiple_of(n * FS, 8), FS)], rwv, load_sem.at[5]
        ),
    ]
    for c in loads:
        c.start()

    def each(count, fn):
        def body(r, carry):
            fn(r)
            return carry

        lax.fori_loop(1, count, body, 0)

    def peer(axis, r):
        me, size = {"group": (g, NG), "inner": (i, NI), "dp": (n, NZ)}[axis]
        return {axis: lax.rem(me + r, size)}

    bar = pltpu.get_barrier_semaphore()
    for axis, size in (("group", NG), ("inner", NI), ("dp", NZ)):
        each(
            size,
            lambda r, axis=axis: pl.semaphore_signal(
                bar, inc=1, device_id=peer(axis, r), device_id_type=MESH
            ),
        )
    pl.semaphore_wait(bar, NG + NI + NZ - 3)

    def remote(src, dst, s, r, dev):
        return pltpu.make_async_remote_copy(
            src_ref=src, dst_ref=dst, send_sem=s, recv_sem=r, device_id=dev, device_id_type=MESH
        )

    def y_copy(t, r):
        src, dst = ((pay1, buf1), (pay2, buf2), (scores, buf3))[t]
        return remote(src, dst.at[g, i], ys.at[t, r], yr.at[t, r], peer("group", r))

    def x_copy(t, r):
        buf = (buf1, buf2, buf3)[t]
        return remote(buf.at[:, i], buf.at[:, i], xs.at[t, r], xr.at[t, r], peer("inner", r))

    each(NG, lambda r: y_copy(0, r).start())
    buf1[g, i] = pay1[...]
    each(NG, lambda r: y_copy(0, r).wait_recv())
    each(NI, lambda r: x_copy(0, r).start())
    each(NG, lambda r: y_copy(1, r).start())
    each(NG, lambda r: y_copy(2, r).start())
    buf2[g, i] = pay2[...]
    buf3[g, i] = scores[...]
    each(NI, lambda r: x_copy(0, r).wait_recv())
    each(NG, lambda r: y_copy(1, r).wait_recv())
    each(NG, lambda r: y_copy(2, r).wait_recv())

    X = buf1[...].reshape(T, FP)
    sel = (iota((16, FP), 1) == iota((16, FP), 0) + FS).astype(bf16)
    codes = dot_nt(sel, X)
    srow = iota((S, T), 0)
    same = (srow >> 1) == (iota((S, T), 1) >> 4)
    for j in range(2):
        want = (2 * q + j + E * (iota((S, 1), 0) & 1)).astype(f32)
        hit = codes[0:1] == want
        for k in range(1, K):
            hit = hit | (codes[k : k + 1] == want)
        pt[pl.ds(j * S, S), :] = jnp.where(same & hit, 1.0, 0.0).astype(bf16)
    xs_rows = dot_nn(pt[...], X)
    xt[n] = xs_rows.T[0:FS].astype(bf16)

    def chunk(c):
        return pl.ds(c * CR, CR)

    def zdev(d):
        return {"dp": lax.rem(n + (1 if d == 0 else NZ - 1), NZ)}

    def ag_copy(d, st, c):
        m = lax.rem(n + (NZ - st if d == 0 else st), NZ)
        ref = xt.at[m, chunk(c)]
        return remote(ref, ref, ag_s.at[d, st, c], ag_r.at[d, st, c], zdev(d))

    def ag_has(d, st, c):
        return st < half - 1 or c == d or CHUNKS == 1

    def transpose_weights(part, parts):
        cols = D // parts
        for j in range(2):
            both = jnp.concatenate(
                (gwv[j, :, part * cols : (part + 1) * cols], uwv[j, :, part * cols : (part + 1) * cols]),
                axis=0,
            )
            wT[j, pl.ds(part * cols, cols), :] = both.astype(f32).T.astype(bf16)

    def fold_saved():
        for j in range(2):
            a = sgv[j].astype(f32)
            u = suv[j].astype(f32)
            sig = jax.nn.sigmoid(a)
            sw = a * sig
            dgu[j, 0] = u * sig * (1.0 + a * (1.0 - sig))
            dgu[j, 1] = sw

    def mix_tokens():
        codes_all = buf2[:, :, :, FP : FP + E].reshape(T, E).astype(f32)
        aff = jax.nn.sigmoid(buf3[...].reshape(T, E))
        named = jnp.where(codes_all > 0.0, aff, 0.0)
        mix = (route_scale * named / jnp.sum(named, axis=1, keepdims=True)).astype(bf16)
        owner = (iota((E, 2 * S), 1) >= S).astype(jnp.int32) + 2 * q
        pick = (iota((E, 2 * S), 0) == owner).astype(bf16)
        spread = dot_nn(mix, pick)
        placed = pt[...].astype(f32).T
        pmix[...] = (placed * spread).astype(bf16).reshape(NG, NI, 16, 2 * S)

    def token_transpose():
        tok = buf2[:, :, :, 0:FP].reshape(T, FP)
        tokT[...] = tok.astype(f32).T[0:FS].astype(bf16)

    parts = 7 if D % (7 * 128) == 0 else half
    for st in range(half):
        for c in range(CHUNKS):
            for d in range(2):
                if st > 0:
                    ag_copy(d, st - 1, c).wait_recv()
                if ag_has(d, st, c):
                    ag_copy(d, st, c).start()
        if st == 0:
            each(NI, lambda r: x_copy(1, r).start())
            each(NI, lambda r: x_copy(2, r).start())
            for c in loads:
                c.wait()
            fold_saved()
        if st == min(2, half - 1):
            each(NI, lambda r: x_copy(1, r).wait_recv())
            each(NI, lambda r: x_copy(2, r).wait_recv())
            mix_tokens()
        if st == min(3, half - 1):
            token_transpose()
        for p in range(parts):
            if p % half == st:
                transpose_weights(p, parts)
    for c in range(CHUNKS):
        for d in range(2):
            if ag_has(d, half - 1, c):
                ag_copy(d, half - 1, c).wait_recv()

    hid = dot_nn(dwv[...].reshape(2 * F, D), xt[...].reshape(D, 2 * S))
    both = []
    for j in range(2):
        h = hid[j * F : (j + 1) * F, j * S : (j + 1) * S]
        up = h * dgu[j, 1]
        gz[n, pl.ds(j, 1), :] = jnp.sum(up * suv[j].astype(f32), axis=0, keepdims=True)
        both.append(jnp.concatenate((h * dgu[j, 0], up), axis=0).astype(bf16))

    def z_copy(r):
        return remote(gz.at[n], gz.at[n], z_s.at[r], z_r.at[r], peer("dp", r))

    each(NZ, lambda r: z_copy(r).start())

    def part(m, c):
        rows = pl.ds(pl.multiple_of(m * FS + c * CR, 16), CR)
        return jnp.concatenate([dot_nn(wT[j, rows, :], both[j]) for j in range(2)], axis=1)

    def gx_copy(r):
        return remote(bufG.at[g, i], bufG.at[g, i], xs.at[3, r], xr.at[3, r], peer("inner", r))

    def gy_copy(r):
        return remote(bufG.at[g], bufG.at[g], ys.at[3, r], yr.at[3, r], peer("group", r))

    def router_side():
        for b in range(NB):
            gflat[2 * b : 2 * b + 2, :] = bufG[b // NI, b % NI]
        gt[...] = gflat[...].T

        def body(b, carry):
            gb, ib = b // NI, lax.rem(b, NI)
            code = buf2[gb, ib, :, FP : FP + E].astype(f32)
            aff = jax.nn.sigmoid(buf3[gb, ib])
            g0 = gt[pl.ds(2 * b, 1), :]
            g1 = gt[pl.ds(2 * b + 1, 1), :]
            grads = jnp.where(code == 1.0, g0, jnp.where(code == 2.0, g1, 0.0))
            named = jnp.where(code > 0.0, aff, 0.0)
            total = jnp.sum(named, axis=1, keepdims=True)
            weighted = jnp.sum(named * grads, axis=1, keepdims=True)
            lg[b] = route_scale * (grads / total - weighted / (total * total)) * named * (1.0 - aff)
            return carry

        lax.fori_loop(0, NB, body, 0)
        rest = lg[...].reshape(T, E)
        acc = None
        for _ in range(3):
            top = rest.astype(bf16)
            term = dot_nn(tokT[...], top)
            acc = term if acc is None else acc + term
            rest = rest - top.astype(f32)
        out_r[...] = acc

    def rs_copy(d, st, c):
        return remote(
            rs_src.at[d, st, chunk(c)], rs_dst.at[d, st, chunk(c)],
            rs_s.at[d, st, c], rs_r.at[d, st, c], zdev(d),
        )

    def rs_has(d, st, c):
        return st > 0 or c == d or CHUNKS == 1

    def rs_step(st, c, d):
        if not rs_has(d, st, c):
            return
        m = lax.rem(n + (half - st if d == 0 else NZ - half + st), NZ)
        acc = part(m, c)
        if st > 0 and rs_has(d, st - 1, c):
            rs_copy(d, st - 1, c).wait_recv()
            acc = acc + rs_dst[d, st - 1, chunk(c), :].astype(f32)
        rs_src[d, st, chunk(c), :] = acc.astype(bf16)
        rs_copy(d, st, c).start()

    for st in range(half):
        for c in range(CHUNKS):
            for d in range(2):
                rs_step(st, c if st else 1 - c, d)
        if st == min(1, half - 1):
            each(NZ, lambda r: z_copy(r).wait_recv())
            bufG[g, i] = jnp.sum(gz[...], axis=0)
            each(NI, lambda r: gx_copy(r).start())
        if st == min(3, half - 1):
            each(NI, lambda r: gx_copy(r).wait_recv())
            each(NG, lambda r: gy_copy(r).start())
        if st == min(5, half - 1):
            each(NG, lambda r: gy_copy(r).wait_recv())
            router_side()

    for c in range(CHUNKS):
        acc = part(n, c)
        for d in range(2):
            if rs_has(d, half - 1, c):
                rs_copy(d, half - 1, c).wait_recv()
                acc = acc + rs_dst[d, half - 1, chunk(c), :].astype(f32)
        finv[chunk(c), :] = acc.astype(bf16)
    if FP > FS:
        finv[FS:FP, :] = jnp.zeros((FP - FS, 2 * S), bf16)

    def tx_copy(r):
        return remote(tbuf.at[r], rbuf.at[r], xs.at[4, r], xr.at[4, r], peer("inner", r))

    def ty_copy(r):
        to = lax.rem(g + r, NG)
        return remote(ysrc.at[to], ydst.at[r], ys.at[4, r], yr.at[4, r], peer("group", r))

    def token_rows(at):
        return dot_nt(pmix[:, at].reshape(NG * 16, 2 * S), finv[...])

    def send_rows(r):
        tbuf[r] = token_rows(lax.rem(i + r, NI)).astype(bf16).reshape(NG, 16, FP)
        tx_copy(r).start()

    each(NI, send_rows)
    acc = token_rows(i)
    extra = dot_nt(lg[q], rwv[...], precision=HI)
    for r in range(1, NI):
        tx_copy(r).wait_recv()
        acc = acc + rbuf[r].astype(f32).reshape(NG * 16, FP)
    yacc[...] = acc.reshape(NG, 16, FP)
    ysrc[...] = acc.astype(bf16).reshape(NG, 16, FP)
    each(NG, lambda r: ty_copy(r).start())
    total = yacc[g]
    for r in range(1, NG):
        ty_copy(r).wait_recv()
        total = total + ydst[r].astype(f32)
    out_x[...] = (total[:, 0:FS] + extra).astype(bf16)

    for t in range(3):
        each(NG, lambda r, t=t: y_copy(t, r).wait_send())
        each(NI, lambda r, t=t: x_copy(t, r).wait_send())
    each(NZ, lambda r: z_copy(r).wait_send())
    each(NI, lambda r: gx_copy(r).wait_send())
    each(NG, lambda r: gy_copy(r).wait_send())
    each(NI, lambda r: tx_copy(r).wait_send())
    each(NG, lambda r: ty_copy(r).wait_send())
    for st in range(half):
        for c in range(CHUNKS):
            for d in range(2):
                if ag_has(d, st, c):
                    ag_copy(d, st, c).wait_send()
                if rs_has(d, st, c):
                    rs_copy(d, st, c).wait_send()


def local(
    token_inputs, out_grads, expert_ids, router_weight,
    gate_weight, up_weight, down_weight, saved_gate, saved_up,
):
    NG, NI, NZ = lax.axis_size("group"), lax.axis_size("inner"), lax.axis_size("dp")
    NB = NG * NI
    tokens, D = token_inputs.shape
    E = router_weight.shape[1]
    K = expert_ids.shape[1]
    F = down_weight.shape[1]
    S = saved_gate.shape[1]
    T = NB * tokens
    FS = D // NZ
    FP = -(-(FS + K) // 128) * 128
    half = NZ // 2
    n = lax.axis_index("dp")

    matches = (expert_ids[:, :, None] == jnp.arange(E, dtype=jnp.int32)).astype(jnp.int32)
    per_token = jnp.sum(matches, axis=1)
    earlier = jnp.cumsum(per_token, axis=0) - per_token
    position = jnp.sum(matches * earlier[:, None, :], axis=2)
    codes = (expert_ids + E * position).astype(bf16)
    code_rows = (per_token * (1 + earlier)).astype(bf16)
    grad_cols = lax.dynamic_slice_in_dim(out_grads, n * FS, FS, 1)
    tok_cols = lax.dynamic_slice_in_dim(token_inputs, n * FS, FS, 1)
    pay1 = jnp.concatenate((grad_cols, codes, jnp.zeros((tokens, FP - FS - K), bf16)), axis=1)
    pay2 = jnp.concatenate((tok_cols, jnp.zeros((tokens, FP - FS), bf16), code_rows), axis=1)
    scores = jnp.dot(token_inputs.astype(f32), router_weight, precision=HI)

    vmem = pl.BlockSpec(memory_space=pltpu.VMEM)
    hbm = pl.BlockSpec(memory_space=pl.ANY)
    V = pltpu.VMEM
    dma = pltpu.SemaphoreType.DMA
    scratch = [
        V((2, F, D), bf16), V((2, F, D), bf16), V((2, F, D), bf16),
        V((2, F, S), bf16), V((2, F, S), bf16), V((FS, E), f32),
        V((NG, NI, 16, FP), bf16), V((NG, NI, 16, FP + E), bf16), V((NG, NI, 16, E), f32),
        V((2 * S, T), bf16), V((NG, NI, 16, 2 * S), bf16), V((2, D, 2 * F), bf16),
        V((FS, T), bf16), V((NZ, FS, 2 * S), bf16), V((2, 2, F, S), f32),
        V((NZ, 2, S), f32), V((NG, NI, 2, S), f32), V((E, S), f32), V((S, E), f32),
        V((NB, 16, E), f32),
        V((2, half, FS, 2 * S), bf16), V((2, half, FS, 2 * S), bf16), V((FP, 2 * S), bf16),
        V((NI, NG, 16, FP), bf16), V((NI, NG, 16, FP), bf16), V((NG, 16, FP), bf16),
        V((NG, 16, FP), f32), V((NG, 16, FP), bf16),
        dma((6,)), dma((5, NG)), dma((5, NG)), dma((5, NI)), dma((5, NI)),
        dma((2, half, CHUNKS)), dma((2, half, CHUNKS)),
        dma((2, half, CHUNKS)), dma((2, half, CHUNKS)),
        dma((NZ,)), dma((NZ,)),
    ]
    return pl.pallas_call(
        functools.partial(kernel, NZ, NG, NI, K),
        out_shape=(
            jax.ShapeDtypeStruct((tokens, FS), bf16),
            jax.ShapeDtypeStruct((FS, E), f32),
        ),
        in_specs=[vmem] * 3 + [hbm] * 6,
        out_specs=(vmem, vmem),
        scratch_shapes=scratch,
        compiler_params=pltpu.CompilerParams(
            collective_id=0, has_side_effects=True, vmem_limit_bytes=40 * 1024 * 1024
        ),
        name="expert_backward",
    )(
        pay1, pay2, scores, router_weight,
        jnp.swapaxes(gate_weight, 1, 2), jnp.swapaxes(up_weight, 1, 2), down_weight,
        jnp.swapaxes(saved_gate, 1, 2), jnp.swapaxes(saved_up, 1, 2),
    )


def solution(mesh):
    placed = (
        P(("group", "inner"), None),
        P(("group", "inner"), None),
        P(("group", "inner"), None),
        P(),
        P(("group", "inner"), None, "dp"),
        P(("group", "inner"), None, "dp"),
        P(("group", "inner"), "dp", None),
        P(("group", "inner"), None, "dp"),
        P(("group", "inner"), None, "dp"),
    )
    return jax.shard_map(
        local,
        mesh=mesh,
        in_specs=placed,
        out_specs=(P(("group", "inner"), "dp"), P("dp", None)),
        check_vma=False,
    )
```

time: 380 us -> 135 us (0.36)
  waiting for transfers between devices: 254 us -> 0 us
  Pallas kernels: 0 us -> 125 us
  starting transfers between devices: 33.7 us -> 0 us
  blocking collectives: 32.2 us -> 0 us
  local copies, waits for them, and re-layouts: 30.1 us -> 6.62 us
  between operations: 15.7 us -> 0.72 us
  matrix products: 11.1 us -> 2.26 us
    psum x1 -> x0, waiting for transfers between devices: 142 us -> none  [local(): router_grad = lax.psum(router_part, ('group', 'inner'))]
    pallas_call x0 -> x1, Pallas kernels: none -> 125 us  [local(): pl.pallas_call(functools.partial(kernel, NZ, NG, NI, K), out_shape=(jax.S...]
    unnamed x3 -> x0, waiting for transfers between devices: 61.8 us -> none
    all_to_all x3 -> x0, waiting for transfers between devices: 50.6 us -> none  [the longest x1 39.8 us: local(): lax.all_to_all(outgoing, ('group', 'inner'), split_axis=0, concat_axis=0,...]
    all_to_all x3 -> x0, starting transfers between devices: 33.6 us -> none  [the longest x1 19.2 us: local(): lax.all_to_all(outgoing, ('group', 'inner'), split_axis=0, concat_axis=0,...]
    psum x1 -> x0, blocking collectives: 32.2 us -> none  [local(): gate_total = lax.psum(gate_partial, 'dp')]
    reshape x3 -> x0, local copies, waits for them, and re-layouts: 9.84 us -> none  [the longest x1 4.91 us: local(): rows_home = rows_home.reshape(experts_all * capacity, model_width)]
    dot_general x6 -> x1, matrix products: 11.1 us -> 2.26 us  [local(): scores = jnp.dot(token_inputs.astype(f32), router_weight, precision=HI)]
  transfers between devices with their start and end apart: 5 -> 0, of which waited for: 5 -> 0; matrix products, arithmetic and copies ran while one was open for 5% -> 0% of each run, Pallas kernels for 0% -> 0%
where the time goes in v1:
time: 135 us
  Pallas kernels  125 us (93%)
  local copies, waits for them, and re-layouts  6.62 us (5%)
  matrix products  2.26 us (2%)
    pallas_call x1, Pallas kernels, local(): pl.pallas_call(functools.partial(kernel, NZ, NG, NI, K), out_shape=(jax.S...  125 us
    unnamed x15, local copies, waits for them, and re-layouts  5.65 us

profile of v1, /device:TPU:1, one launch (start us, length us, event | category | flops | bytes accessed | tf_op | source)
XLA Modules:
  0.0 134.8 jit_solution(14480179646782592977)
XLA Ops:
  0.6 0.0 copy-start
  0.6 0.0 copy-start.5
  0.7 0.0 copy-start.4
  0.7 0.1 pad.1.clone
  0.8 0.1 pad.5.clone
  0.8 0.9 copy.14
  1.7 0.1 convert_reduce_fusion
  1.8 0.4 select_reduce_fusion
  2.3 2.3 %fusion.scores = f32[16,128]{1,0:T(8,128)S(1)} fusion(bf16[16,3584]{1,0:T(8,128)(2,1)} %param.9, f32[3584,128]{1,0:T(8,128)} %rw_hbm.1), kind=kOutput, calls=%fused_computation.9 | convolution fusion | flops 88080384 | bytes 1957888 | tf_op jit(solution)/shard_map/dot_general | solution.py:368
  4.5 0.8 constant_dynamic-slice_fusion
  5.4 0.1 maximum_maximum_fusion.pay1
  5.4 0.0 copy-done
  5.4 0.0 copy-done.5
  5.4 0.0 copy-done.4
  5.4 0.0 copy-start.1
  5.5 1.2 copy-done.1
  6.6 0.0 copy-start.2
  6.6 1.2 copy-done.2
  7.8 0.0 copy-start.3
  7.8 1.2 copy-done.3
  9.0 124.5 %expert_backward.1 = (bf16[16,224]{1,0:T(8,128)(2,1)S(1)}, f32[224,128]{1,0:T(8,128)S(1)}) custom-call(bf16[16,256]{1,0:T(8,128)(2,1)S(1)} %maximum_maximum_fusion.pay1, bf16[16,384]{1,0:T(8,128)(2,1)S(1)} %pad_maximum_fusion.pay2, f32[16,128]{1,0:T(8,128)S(1)} %fusion.scores, f32[3584,128]{1,0:T(8,128)S(1)} %copy-done, bf16[2,64,3584]{2,1,0:T(8,128)(2,1)S(1)} %bitcast.6, ...), custom_call_target="tpu_custom_call" | custom-call | tf_op jit(solution)/shard_map/expert_backward/pallas_call | solution.py:390
  133.5 0.6 copy.17
  134.1 0.6 copy.18
  (6 shorter events, 0.1 us)
Async XLA Ops:
  0.6 4.8 %copy-start = (f32[3584,128]{1,0:T(8,128)S(1)}, f32[3584,128]{1,0:T(8,128)}, u32[]{:S(2)}) copy-start(f32[3584,128]{1,0:T(8,128)} %rw_hbm.1) | copy-start | bytes 5505028
  0.6 4.8 %copy-start.5 = (bf16[2,128,64]{1,2,0:T(8,128)(2,1)S(1)}, bf16[2,128,64]{1,2,0:T(8,128)(2,1)}, u32[]{:S(2)}) copy-start(bf16[2,128,64]{1,2,0:T(8,128)(2,1)} %param.17) | copy-start | bytes 98308
  0.7 4.8 %copy-start.4 = (bf16[2,128,64]{1,2,0:T(8,128)(2,1)S(1)}, bf16[2,128,64]{1,2,0:T(8,128)(2,1)}, u32[]{:S(2)}) copy-start(bf16[2,128,64]{1,2,0:T(8,128)(2,1)} %param.16) | copy-start | bytes 98308
  5.4 1.2 copy-start.1
  6.6 1.2 copy-start.2
  7.8 1.2 copy-start.3

commit v2 on v1

v2 whole, which is shorter than its diff:
```python
import functools

import jax
import jax.numpy as jnp
from jax import lax
from jax.experimental import pallas as pl
from jax.experimental.pallas import tpu as pltpu
from jax.sharding import PartitionSpec as P

MESH = pl.DeviceIdType.MESH
route_scale = 2.5
f32, bf16 = jnp.float32, jnp.bfloat16
HI = lax.Precision.HIGHEST


def dot_nt(a, b, **kw):
    return lax.dot_general(a, b, (((1,), (1,)), ((), ())), preferred_element_type=f32, **kw)


def dot_nn(a, b):
    return lax.dot_general(a, b, (((1,), (0,)), ((), ())), preferred_element_type=f32)


def iota(shape, dim):
    return lax.broadcasted_iota(jnp.int32, shape, dim)


def kernel(
    NZ, NG, NI, K,
    pay1, pay2, tok, rw_hbm, gw_hbm, uw_hbm, dw_hbm, sg_hbm, su_hbm,
    out_x, out_r,
    gwv, uwv, dwv, sgv, suv, rwv, dws,
    buf1, buf2, buf3, pt, pmix, wT, tokT, xt, dgu, gz, bufG, gflat, gt, lg,
    rs_src, rs_dst, finv, tbuf, rbuf, ysrc, yacc, ydst,
    load_sem, ys, yr, xs, xr, ag_s, ag_r, rs_s, rs_r, z_s, z_r,
):
    NB = NG * NI
    T = 16 * NB
    S = 2 * NB
    E = 2 * NB
    FP = pay1.shape[1]
    F = dwv.shape[1]
    D = dwv.shape[2]
    FS = D // NZ
    half = NZ // 2
    CR = FS // 2
    g, i, n = lax.axis_index("group"), lax.axis_index("inner"), lax.axis_index("dp")
    q = g * NI + i

    load_rw = pltpu.make_async_copy(rw_hbm, rwv, load_sem.at[0])
    loads = [
        pltpu.make_async_copy(dw_hbm, dwv, load_sem.at[1]),
        pltpu.make_async_copy(sg_hbm, sgv, load_sem.at[2]),
        pltpu.make_async_copy(su_hbm, suv, load_sem.at[3]),
    ]
    loads_w = [
        pltpu.make_async_copy(gw_hbm, gwv, load_sem.at[4]),
        pltpu.make_async_copy(uw_hbm, uwv, load_sem.at[5]),
    ]

    def each(count, fn):
        def body(r, carry):
            fn(r)
            return carry

        lax.fori_loop(1, count, body, 0)

    def peer(axis, r):
        me, size = {"group": (g, NG), "inner": (i, NI), "dp": (n, NZ)}[axis]
        return {axis: lax.rem(me + r, size)}

    bar = pltpu.get_barrier_semaphore()
    for axis, offsets in (("dp", (1, NZ - 1)), ("group", range(1, NG)), ("inner", range(1, NI))):
        for r in offsets:
            pl.semaphore_signal(bar, inc=1, device_id=peer(axis, r), device_id_type=MESH)
    load_rw.start()
    for c in loads + loads_w:
        c.start()
    pl.semaphore_wait(bar, NG + NI)

    def remote(src, dst, s, r, dev):
        return pltpu.make_async_remote_copy(
            src_ref=src, dst_ref=dst, send_sem=s, recv_sem=r, device_id=dev, device_id_type=MESH
        )

    def y_copy(t, r):
        src, dst = ((pay1, buf1), (pay2, buf2), (None, buf3))[t]
        src = buf3.at[g, i] if src is None else src
        return remote(src, dst.at[g, i], ys.at[t], yr.at[t], peer("group", r))

    def y_all(t):
        ref = (buf1, buf2, buf3)[t].at[pl.ds(0, NG - 1), i]
        return remote(ref, ref, ys.at[t], yr.at[t], peer("group", 1))

    def x_copy(t, r):
        buf = (buf1, buf2, buf3)[t]
        return remote(buf.at[:, i], buf.at[:, i], xs.at[t], xr.at[t], peer("inner", r))

    def x_all(t):
        ref = (buf1, buf2, buf3)[t].at[:, pl.ds(0, NI - 1)]
        return remote(ref, ref, xs.at[t], xr.at[t], peer("inner", 1))

    each(NG, lambda r: y_copy(0, r).start())
    buf1[g, i] = pay1[...]
    each(NG, lambda r: y_copy(1, r).start())
    buf2[g, i] = pay2[...]
    load_rw.wait()
    parts = 7 if D % (7 * 128) == 0 else half
    cols = D // parts
    scores = None
    for p in range(parts):
        rest = rwv[p * cols : (p + 1) * cols, :]
        left = tok[:, p * cols : (p + 1) * cols]
        for _ in range(3):
            top = rest.astype(bf16)
            term = dot_nn(left, top)
            scores = term if scores is None else scores + term
            rest = rest - top.astype(f32)
    buf3[g, i] = scores
    each(NG, lambda r: y_copy(2, r).start())
    for c in loads:
        c.wait()
    for j in range(2):
        a = sgv[j].astype(f32)
        u = suv[j].astype(f32)
        sig = jax.nn.sigmoid(a)
        dgu[j, 0] = u * sig * (1.0 + a * (1.0 - sig))
        dgu[j, 1] = a * sig

    y_all(0).wait_recv()
    each(NI, lambda r: x_copy(0, r).start())
    down = dwv[...].reshape(2 * F, D)
    for m in range(NZ):
        dws[m, :, 0:FS] = down[:, m * FS : (m + 1) * FS]
    for c in loads_w:
        c.wait()
    for p in range(parts):
        cut = slice(p * cols, (p + 1) * cols)
        rows = jnp.concatenate((gwv[0, :, cut], uwv[0, :, cut], gwv[1, :, cut], uwv[1, :, cut]), axis=0)
        wT[cut, :] = rows.astype(f32).T.astype(bf16)
    x_all(0).wait_recv()

    X = buf1[...].reshape(T, FP)
    sel = (iota((16, FP), 1) == iota((16, FP), 0) + FS).astype(bf16)
    codes = dot_nt(sel, X)
    srow = iota((S, T), 0)
    same = (srow >> 1) == (iota((S, T), 1) >> 4)
    for j in range(2):
        want = (2 * q + j + E * (iota((S, 1), 0) & 1)).astype(f32)
        hit = codes[0:1] == want
        for k in range(1, K):
            hit = hit | (codes[k : k + 1] == want)
        pt[pl.ds(j * S, S), :] = jnp.where(same & hit, 1.0, 0.0).astype(bf16)
    xs_rows = dot_nn(pt[...], X)
    xt[n] = xs_rows.T[0:FS].astype(bf16)

    def rows_of(c):
        return pl.ds((c // 2) * CR, CR)

    def lanes_of(c):
        return pl.ds((c % 2) * S, S)

    def zdev(d):
        return {"dp": lax.rem(n + (1 if d == 0 else NZ - 1), NZ)}

    def behind(d, st):
        return lax.rem(n + (NZ - st if d == 0 else st), NZ)

    def ag_copy(d, st, c):
        ref = xt.at[behind(d, st), rows_of(c), lanes_of(c)]
        return remote(ref, ref, ag_s.at[d, c], ag_r.at[d, st, c], zdev(d))

    def ag_sent(d, c):
        ref = xt.at[pl.ds(0, half if c // 2 == d else half - 1), rows_of(c), lanes_of(c)]
        return remote(ref, ref, ag_s.at[d, c], ag_r.at[d, 0, c], zdev(d))

    def ag_has(d, st, c):
        return st < half - 1 or c // 2 == d

    def mix_tokens():
        codes_all = buf2[:, :, :, FP : FP + E].reshape(T, E).astype(f32)
        aff = jax.nn.sigmoid(buf3[...].reshape(T, E))
        named = jnp.where(codes_all > 0.0, aff, 0.0)
        mix = (route_scale * named / jnp.sum(named, axis=1, keepdims=True)).astype(bf16)
        owner = (iota((E, 2 * S), 1) >= S).astype(jnp.int32) + 2 * q
        pick = (iota((E, 2 * S), 0) == owner).astype(bf16)
        spread = dot_nn(mix, pick)
        placed = pt[...].astype(f32).T
        pmix[...] = (placed * spread).astype(bf16).reshape(NG, NI, 16, 2 * S)

    def token_transpose():
        rows = buf2[:, :, :, 0:FP].reshape(T, FP)
        tokT[...] = rows.astype(f32).T[0:FS].astype(bf16)

    def hidden_term(m):
        return dot_nn(dws[m, :, 0:FS], xt[m])

    hid = None
    for st in range(half):
        for c in range(4):
            for d in range(2):
                if st > 0:
                    ag_copy(d, st - 1, c).wait_recv()
                if ag_has(d, st, c):
                    ag_copy(d, st, c).start()
        if st == 0:
            y_all(1).wait_recv()
            y_all(2).wait_recv()
            each(NI, lambda r: x_copy(1, r).start())
            each(NI, lambda r: x_copy(2, r).start())
            hid = hidden_term(n)
        else:
            hid = hid + hidden_term(behind(0, st)) + hidden_term(behind(1, st))
        if st == min(3, half - 1):
            x_all(1).wait_recv()
            x_all(2).wait_recv()
            mix_tokens()
        if st == min(4, half - 1):
            token_transpose()
    for d in range(2):
        for c in range(4):
            if ag_has(d, half - 1, c):
                ag_copy(d, half - 1, c).wait_recv()
    hid = hid + hidden_term(behind(0, half))

    both = []
    for j in range(2):
        h = hid[j * F : (j + 1) * F, j * S : (j + 1) * S]
        up = h * dgu[j, 1]
        gz[n, pl.ds(j, 1), :] = jnp.sum(up * suv[j].astype(f32), axis=0, keepdims=True)
        pair = jnp.concatenate((h * dgu[j, 0], up), axis=0).astype(bf16)
        none = jnp.zeros_like(pair)
        both.append(jnp.concatenate((pair, none) if j == 0 else (none, pair), axis=1))
    grads_t = jnp.concatenate(both, axis=0)

    def part(m):
        return dot_nn(wT[pl.ds(pl.multiple_of(m * FS, 16), FS), :], grads_t)

    def z_copy(d, st):
        ref = gz.at[behind(d, st)]
        return remote(ref, ref, z_s.at[d], z_r.at[d, st], zdev(d))

    def z_sent(d):
        ref = gz.at[pl.ds(0, half - d)]
        return remote(ref, ref, z_s.at[d], z_r.at[d, 0], zdev(d))

    def gx_copy(r):
        return remote(bufG.at[g, i], bufG.at[g, i], xs.at[3], xr.at[3], peer("inner", r))

    def gx_all():
        ref = bufG.at[g, pl.ds(0, NI - 1)]
        return remote(ref, ref, xs.at[3], xr.at[3], peer("inner", 1))

    def gy_copy(r):
        return remote(bufG.at[g], bufG.at[g], ys.at[3], yr.at[3], peer("group", r))

    def gy_all():
        ref = bufG.at[pl.ds(0, NG - 1)]
        return remote(ref, ref, ys.at[3], yr.at[3], peer("group", 1))

    def router_side():
        for b in range(NB):
            gflat[2 * b : 2 * b + 2, :] = bufG[b // NI, b % NI]
        gt[...] = gflat[...].T

        def body(b, carry):
            gb, ib = b // NI, lax.rem(b, NI)
            code = buf2[gb, ib, :, FP : FP + E].astype(f32)
            aff = jax.nn.sigmoid(buf3[gb, ib])
            g0 = gt[pl.ds(2 * b, 1), :]
            g1 = gt[pl.ds(2 * b + 1, 1), :]
            grads = jnp.where(code == 1.0, g0, jnp.where(code == 2.0, g1, 0.0))
            named = jnp.where(code > 0.0, aff, 0.0)
            total = jnp.sum(named, axis=1, keepdims=True)
            weighted = jnp.sum(named * grads, axis=1, keepdims=True)
            lg[b] = route_scale * (grads / total - weighted / (total * total)) * named * (1.0 - aff)
            return carry

        lax.fori_loop(0, NB, body, 0, unroll=8)

    def router_product():
        rest = lg[...].reshape(T, E)
        acc = None
        for _ in range(3):
            top = rest.astype(bf16)
            term = dot_nn(tokT[...], top)
            acc = term if acc is None else acc + term
            rest = rest - top.astype(f32)
        out_r[...] = acc

    def rs_copy(d, st, c):
        return remote(
            rs_src.at[d, st, rows_of(c), lanes_of(c)], rs_dst.at[d, st, rows_of(c), lanes_of(c)],
            rs_s.at[d, c], rs_r.at[d, st, c], zdev(d),
        )

    def rs_sent(d, c):
        cut = (d, pl.ds(0, half if c // 2 == d else half - 1), rows_of(c), lanes_of(c))
        return remote(rs_src.at[cut], rs_dst.at[cut], rs_s.at[d, c], rs_r.at[d, 0, c], zdev(d))

    def rs_has(d, st, c):
        return st > 0 or c // 2 == d

    def cut_of(value, c):
        return value[(c // 2) * CR : (c // 2 + 1) * CR, (c % 2) * S : (c % 2 + 1) * S]

    for st in range(half):
        ahead = [part(behind(1 - d, half - st)) for d in range(2)] if st else [part(behind(0, half))] * 2
        for d in range(2):
            if st > 0:
                z_copy(d, st - 1).wait_recv()
            if st < half - d:
                z_copy(d, st).start()
        for cc in range(4):
            for d in range(2):
                c = cc if d == 0 else (cc + 2) % 4
                if not rs_has(d, st, c):
                    continue
                acc = cut_of(ahead[d], c)
                if st > 0 and rs_has(d, st - 1, c):
                    rs_copy(d, st - 1, c).wait_recv()
                    acc = acc + rs_dst[d, st - 1, rows_of(c), lanes_of(c)].astype(f32)
                rs_src[d, st, rows_of(c), lanes_of(c)] = acc.astype(bf16)
                rs_copy(d, st, c).start()

    mine = part(n)
    z_copy(0, half - 1).wait_recv()
    bufG[g, i] = jnp.sum(gz[...], axis=0)
    each(NI, lambda r: gx_copy(r).start())
    for c in range(4):
        acc = cut_of(mine, c)
        for d in range(2):
            if rs_has(d, half - 1, c):
                rs_copy(d, half - 1, c).wait_recv()
                acc = acc + rs_dst[d, half - 1, rows_of(c), lanes_of(c)].astype(f32)
        finv[rows_of(c), lanes_of(c)] = acc.astype(bf16)
    if FP > FS:
        finv[FS:FP, :] = jnp.zeros((FP - FS, 2 * S), bf16)

    def tx_copy(r):
        return remote(tbuf.at[r], rbuf.at[r], xs.at[4], xr.at[4], peer("inner", r))

    def tx_all():
        cut = pl.ds(1, NI - 1)
        return remote(tbuf.at[cut], rbuf.at[cut], xs.at[4], xr.at[4], peer("inner", 1))

    def ty_copy(r):
        to = lax.rem(g + r, NG)
        return remote(ysrc.at[to], ydst.at[r], ys.at[4], yr.at[4], peer("group", r))

    def ty_all():
        return remote(
            ysrc.at[pl.ds(0, NG - 1)], ydst.at[pl.ds(1, NG - 1)], ys.at[4], yr.at[4], peer("group", 1)
        )

    def token_rows(at):
        return dot_nt(pmix[:, at].reshape(NG * 16, 2 * S), finv[...])

    def send_rows(r):
        tbuf[r] = token_rows(lax.rem(i + r, NI)).astype(bf16).reshape(NG, 16, FP)
        tx_copy(r).start()

    each(NI, send_rows)
    acc = token_rows(i)
    gx_all().wait_recv()
    each(NG, lambda r: gy_copy(r).start())
    tx_all().wait_recv()
    for r in range(1, NI):
        acc = acc + rbuf[r].astype(f32).reshape(NG * 16, FP)
    yacc[...] = acc.reshape(NG, 16, FP)
    ysrc[...] = acc.astype(bf16).reshape(NG, 16, FP)
    each(NG, lambda r: ty_copy(r).start())
    gy_all().wait_recv()
    router_side()
    extra = dot_nt(lg[q], rwv[pl.ds(pl.multiple_of(n * FS, 8), FS), :], precision=HI)
    router_product()
    total = yacc[g]
    ty_all().wait_recv()
    for r in range(1, NG):
        total = total + ydst[r].astype(f32)
    out_x[...] = (total[:, 0:FS] + extra).astype(bf16)

    for t in range(3):
        y_all(t).wait_send()
        x_all(t).wait_send()
    gx_all().wait_send()
    gy_all().wait_send()
    tx_all().wait_send()
    ty_all().wait_send()
    for d in range(2):
        z_sent(d).wait_send()
        for c in range(4):
            ag_sent(d, c).wait_send()
            rs_sent(d, c).wait_send()


def local(
    token_inputs, out_grads, expert_ids, router_weight,
    gate_weight, up_weight, down_weight, saved_gate, saved_up,
):
    NG, NI, NZ = lax.axis_size("group"), lax.axis_size("inner"), lax.axis_size("dp")
    NB = NG * NI
    tokens, D = token_inputs.shape
    E = router_weight.shape[1]
    K = expert_ids.shape[1]
    F = down_weight.shape[1]
    S = saved_gate.shape[1]
    T = NB * tokens
    FS = D // NZ
    FP = -(-(FS + K) // 128) * 128
    half = NZ // 2
    n = lax.axis_index("dp")

    matches = (expert_ids[:, :, None] == jnp.arange(E, dtype=jnp.int32)).astype(jnp.int32)
    per_token = jnp.sum(matches, axis=1)
    earlier = jnp.cumsum(per_token, axis=0) - per_token
    position = jnp.sum(matches * earlier[:, None, :], axis=2)
    codes = (expert_ids + E * position).astype(bf16)
    code_rows = (per_token * (1 + earlier)).astype(bf16)
    grad_cols = lax.dynamic_slice_in_dim(out_grads, n * FS, FS, 1)
    tok_cols = lax.dynamic_slice_in_dim(token_inputs, n * FS, FS, 1)
    pay1 = jnp.concatenate((grad_cols, codes, jnp.zeros((tokens, FP - FS - K), bf16)), axis=1)
    pay2 = jnp.concatenate((tok_cols, jnp.zeros((tokens, FP - FS), bf16), code_rows), axis=1)

    vmem = pl.BlockSpec(memory_space=pltpu.VMEM)
    hbm = pl.BlockSpec(memory_space=pl.ANY)
    V = pltpu.VMEM
    dma = pltpu.SemaphoreType.DMA
    scratch = [
        V((2, F, D), bf16), V((2, F, D), bf16), V((2, F, D), bf16),
        V((2, F, S), bf16), V((2, F, S), bf16), V((D, E), f32), V((NZ, 2 * F, FP), bf16),
        V((NG, NI, 16, FP), bf16), V((NG, NI, 16, FP + E), bf16), V((NG, NI, 16, E), f32),
        V((2 * S, T), bf16), V((NG, NI, 16, 2 * S), bf16), V((D, 4 * F), bf16),
        V((FS, T), bf16), V((NZ, FS, 2 * S), bf16), V((2, 2, F, S), f32),
        V((NZ, 2, S), f32), V((NG, NI, 2, S), f32), V((E, S), f32), V((S, E), f32),
        V((NB, 16, E), f32),
        V((2, half, FS, 2 * S), bf16), V((2, half, FS, 2 * S), bf16), V((FP, 2 * S), bf16),
        V((NI, NG, 16, FP), bf16), V((NI, NG, 16, FP), bf16), V((NG, 16, FP), bf16),
        V((NG, 16, FP), f32), V((NG, 16, FP), bf16),
        dma((6,)), dma((5,)), dma((5,)), dma((5,)), dma((5,)),
        dma((2, 4)), dma((2, half, 4)), dma((2, 4)), dma((2, half, 4)),
        dma((2,)), dma((2, half)),
    ]
    return pl.pallas_call(
        functools.partial(kernel, NZ, NG, NI, K),
        out_shape=(
            jax.ShapeDtypeStruct((tokens, FS), bf16),
            jax.ShapeDtypeStruct((FS, E), f32),
        ),
        in_specs=[vmem] * 3 + [hbm] * 6,
        out_specs=(vmem, vmem),
        scratch_shapes=scratch,
        compiler_params=pltpu.CompilerParams(
            collective_id=0, has_side_effects=True, vmem_limit_bytes=58 * 1024 * 1024
        ),
        name="expert_backward",
    )(
        pay1, pay2, token_inputs, router_weight,
        jnp.swapaxes(gate_weight, 1, 2), jnp.swapaxes(up_weight, 1, 2), down_weight,
        jnp.swapaxes(saved_gate, 1, 2), jnp.swapaxes(saved_up, 1, 2),
    )


def solution(mesh):
    placed = (
        P(("group", "inner"), None),
        P(("group", "inner"), None),
        P(("group", "inner"), None),
        P(),
        P(("group", "inner"), None, "dp"),
        P(("group", "inner"), None, "dp"),
        P(("group", "inner"), "dp", None),
        P(("group", "inner"), None, "dp"),
        P(("group", "inner"), None, "dp"),
    )
    return jax.shard_map(
        local,
        mesh=mesh,
        in_specs=placed,
        out_specs=(P(("group", "inner"), "dp"), P("dp", None)),
        check_vma=False,
    )
```

time: 135 us -> 118 us (0.87)
  Pallas kernels: 125 us -> 110 us
  matrix products: 2.26 us -> 0 us
  local copies, waits for them, and re-layouts: 6.62 us -> 4.58 us
    pallas_call x1, Pallas kernels: 125 us -> 110 us  [local(): pl.pallas_call(functools.partial(kernel, NZ, NG, NI, K), out_shape=(jax.S...]
    dot_general x1 -> x0, matrix products: 2.26 us -> none  [local(): scores = jnp.dot(token_inputs.astype(f32), router_weight, precision=HI)]
    unnamed x15 -> x3, local copies, waits for them, and re-layouts: 5.65 us -> 3.6 us
where the time goes in v2:
time: 118 us; the launch traced here: 117 us
  Pallas kernels  110 us (93%)
  local copies, waits for them, and re-layouts  4.58 us (4%)
  other arithmetic  1.84 us (2%)
    pallas_call x1, Pallas kernels, local(): pl.pallas_call(functools.partial(kernel, NZ, NG, NI, K), out_shape=(jax.S...  110 us
    unnamed x3, local copies, waits for them, and re-layouts  3.6 us

profile of v2, /device:TPU:1, one launch (start us, length us, event | category | flops | bytes accessed | tf_op | source)
XLA Modules:
  0.0 117.4 jit_solution(3313304152219424044)
XLA Ops:
  0.6 0.1 pad.1.clone
  0.7 0.1 pad.5.clone
  0.8 0.8 copy.14
  1.6 0.1 convert_reduce_fusion
  1.7 0.4 select_reduce_fusion
  2.1 0.8 constant_dynamic-slice_fusion
  2.9 0.6 pad_maximum_fusion.pay2
  3.6 0.7 maximum_maximum_fusion.pay1
  4.2 110.4 %expert_backward.1 = (bf16[16,224]{1,0:T(8,128)(2,1)}, f32[224,128]{1,0:T(8,128)}) custom-call(bf16[16,256]{1,0:T(8,128)(2,1)} %maximum_maximum_fusion.pay1, bf16[16,384]{1,0:T(8,128)(2,1)} %pad_maximum_fusion.pay2, bf16[16,3584]{1,0:T(8,128)(2,1)} %tok.1, f32[3584,128]{1,0:T(8,128)} %rw_hbm.1, bf16[2,64,3584]{2,1,0:T(8,128)(2,1)} %bitcast.4, ...), custom_call_target="tpu_custom_call" | custom-call | tf_op jit(solution)/shard_map/expert_backward/pallas_call | solution.py:444
  114.6 1.3 %copy.17 = bf16[16,224]{1,0:T(8,128)(2,1)} copy(bf16[16,224]{1,0:T(8,128)(2,1)} %get-tuple-element.8) | data formatting | bytes 14336
  115.9 1.6 %copy.18 = f32[224,128]{1,0:T(8,128)} copy(f32[224,128]{1,0:T(8,128)} %get-tuple-element.9) | data formatting | bytes 229376
  (5 shorter events, 0.1 us)

commit v3 on v2

--- a/solution.py
+++ b/solution.py
@@ -27,7 +27,7 @@
 
 def kernel(
     NZ, NG, NI, K,
-    pay1, pay2, tok, rw_hbm, gw_hbm, uw_hbm, dw_hbm, sg_hbm, su_hbm,
+    ids, grads, tok, rw_hbm, gw_hbm, uw_hbm, dw_hbm, sg_hbm, su_hbm,
     out_x, out_r,
     gwv, uwv, dwv, sgv, suv, rwv, dws,
     buf1, buf2, buf3, pt, pmix, wT, tokT, xt, dgu, gz, bufG, gflat, gt, lg,
@@ -38,12 +38,13 @@
     T = 16 * NB
     S = 2 * NB
     E = 2 * NB
-    FP = pay1.shape[1]
+    FP = buf1.shape[3]
     F = dwv.shape[1]
     D = dwv.shape[2]
     FS = D // NZ
     half = NZ // 2
     CR = FS // 2
+    JUMP = 3 if half >= 5 else 0
     g, i, n = lax.axis_index("group"), lax.axis_index("inner"), lax.axis_index("dp")
     q = g * NI + i
 
@@ -70,13 +71,38 @@
         return {axis: lax.rem(me + r, size)}
 
     bar = pltpu.get_barrier_semaphore()
-    for axis, offsets in (("dp", (1, NZ - 1)), ("group", range(1, NG)), ("inner", range(1, NI))):
+    zpeers = (1, NZ - 1) + ((JUMP, NZ - JUMP) if JUMP else ())
+    for axis, offsets in (("dp", zpeers), ("group", range(1, NG)), ("inner", range(1, NI))):
         for r in offsets:
             pl.semaphore_signal(bar, inc=1, device_id=peer(axis, r), device_id_type=MESH)
     load_rw.start()
     for c in loads + loads_w:
         c.start()
-    pl.semaphore_wait(bar, NG + NI)
+
+    lane_e = iota((16, E), 1).astype(f32)
+    eye = (iota((16, 16), 1) == iota((16, 16), 0)).astype(bf16)
+    named_ids = dot_nt(eye, ids[...].astype(f32).astype(bf16))
+    hits = [named_ids[:, k : k + 1] == lane_e for k in range(K)]
+    per_token = jnp.where(hits[0], 1.0, 0.0)
+    for k in range(1, K):
+        per_token = per_token + jnp.where(hits[k], 1.0, 0.0)
+    lower = (iota((16, 16), 1) < iota((16, 16), 0)).astype(bf16)
+    earlier = dot_nn(lower, per_token.astype(bf16))
+    lane_p = iota((16, FP), 1)
+    turn = lax.rem(D - n * FS, D)
+
+    def columns(ref):
+        return jnp.where(lane_p < FS, pltpu.roll(ref[...].astype(f32), turn, 1)[:, 0:FP], 0.0)
+
+    rows1 = columns(grads)
+    for k in range(K):
+        position = jnp.sum(jnp.where(hits[k], earlier, 0.0), axis=1, keepdims=True)
+        code = named_ids[:, k : k + 1] + E * position
+        rows1 = jnp.where(lane_p == FS + k, code, rows1)
+    buf1[g, i] = rows1.astype(bf16)
+    buf2[g, i, :, 0:FP] = columns(tok).astype(bf16)
+    buf2[g, i, :, FP : FP + E] = (per_token * (1.0 + earlier)).astype(bf16)
+    pl.semaphore_wait(bar, NG + NI - 2 + len(zpeers))
 
     def remote(src, dst, s, r, dev):
         return pltpu.make_async_remote_copy(
@@ -84,9 +110,8 @@
         )
 
     def y_copy(t, r):
-        src, dst = ((pay1, buf1), (pay2, buf2), (None, buf3))[t]
-        src = buf3.at[g, i] if src is None else src
-        return remote(src, dst.at[g, i], ys.at[t], yr.at[t], peer("group", r))
+        ref = (buf1, buf2, buf3)[t].at[g, i]
+        return remote(ref, ref, ys.at[t], yr.at[t], peer("group", r))
 
     def y_all(t):
         ref = (buf1, buf2, buf3)[t].at[pl.ds(0, NG - 1), i]
@@ -101,9 +126,7 @@
         return remote(ref, ref, xs.at[t], xr.at[t], peer("inner", 1))
 
     each(NG, lambda r: y_copy(0, r).start())
-    buf1[g, i] = pay1[...]
     each(NG, lambda r: y_copy(1, r).start())
-    buf2[g, i] = pay2[...]
     load_rw.wait()
     parts = 7 if D % (7 * 128) == 0 else half
     cols = D // parts
@@ -160,22 +183,36 @@
     def lanes_of(c):
         return pl.ds((c % 2) * S, S)
 
-    def zdev(d):
-        return {"dp": lax.rem(n + (1 if d == 0 else NZ - 1), NZ)}
+    def zdev(d, dist):
+        by = dist if dist == JUMP else 1
+        return {"dp": lax.rem(n + (by if d == 0 else NZ - by), NZ)}
 
     def behind(d, st):
         return lax.rem(n + (NZ - st if d == 0 else st), NZ)
 
-    def ag_copy(d, st, c):
-        ref = xt.at[behind(d, st), rows_of(c), lanes_of(c)]
-        return remote(ref, ref, ag_s.at[d, c], ag_r.at[d, st, c], zdev(d))
+    def held(d, dist):
+        return n if dist == JUMP else behind(d, dist - 1)
+
+    if JUMP:
+        chains = [list(range(JUMP, half + 1)), list(range(1, JUMP))]
+    else:
+        chains = [list(range(1, half + 1))]
+    plan = [[(None, ch[0]) for ch in chains]]
+    for st in range(1, len(chains[0]) + 1):
+        plan.append(
+            [(ch[st - 1], ch[st] if st < len(ch) else None) for ch in chains if st <= len(ch)]
+        )
+
+    def ag_copy(d, dist, c):
+        ref = xt.at[held(d, dist), rows_of(c), lanes_of(c)]
+        return remote(ref, ref, ag_s.at[d, c], ag_r.at[d, dist - 1, c], zdev(d, dist))
 
     def ag_sent(d, c):
         ref = xt.at[pl.ds(0, half if c // 2 == d else half - 1), rows_of(c), lanes_of(c)]
-        return remote(ref, ref, ag_s.at[d, c], ag_r.at[d, 0, c], zdev(d))
-
-    def ag_has(d, st, c):
-        return st < half - 1 or c // 2 == d
+        return remote(ref, ref, ag_s.at[d, c], ag_r.at[d, 0, c], zdev(d, 1))
+
+    def ag_has(d, dist, c):
+        return dist < half or c // 2 == d
 
     def mix_tokens():
         codes_all = buf2[:, :, :, FP : FP + E].reshape(T, E).astype(f32)
@@ -196,32 +233,28 @@
         return dot_nn(dws[m, :, 0:FS], xt[m])
 
     hid = None
-    for st in range(half):
-        for c in range(4):
-            for d in range(2):
-                if st > 0:
-                    ag_copy(d, st - 1, c).wait_recv()
-                if ag_has(d, st, c):
-                    ag_copy(d, st, c).start()
+    for st, moves in enumerate(plan):
+        for came, goes in moves:
+            for c in range(4):
+                for d in range(2):
+                    if came is not None and ag_has(d, came, c):
+                        ag_copy(d, came, c).wait_recv()
+                    if goes is not None and ag_has(d, goes, c):
+                        ag_copy(d, goes, c).start()
         if st == 0:
             y_all(1).wait_recv()
             y_all(2).wait_recv()
             each(NI, lambda r: x_copy(1, r).start())
             each(NI, lambda r: x_copy(2, r).start())
             hid = hidden_term(n)
-        else:
-            hid = hid + hidden_term(behind(0, st)) + hidden_term(behind(1, st))
-        if st == min(3, half - 1):
+        for came, goes in moves:
+            if came is not None:
+                hid = hid + hidden_term(behind(0, came))
+                if came < half:
+                    hid = hid + hidden_term(behind(1, came))
+        if st == len(plan) - 2:
             x_all(1).wait_recv()
-            x_all(2).wait_recv()
-            mix_tokens()
-        if st == min(4, half - 1):
             token_transpose()
-    for d in range(2):
-        for c in range(4):
-            if ag_has(d, half - 1, c):
-                ag_copy(d, half - 1, c).wait_recv()
-    hid = hid + hidden_term(behind(0, half))
 
     both = []
     for j in range(2):
@@ -236,13 +269,21 @@
     def part(m):
         return dot_nn(wT[pl.ds(pl.multiple_of(m * FS, 16), FS), :], grads_t)
 
-    def z_copy(d, st):
-        ref = gz.at[behind(d, st)]
-        return remote(ref, ref, z_s.at[d], z_r.at[d, st], zdev(d))
+    def z_copy(d, dist):
+        ref = gz.at[held(d, dist)]
+        return remote(ref, ref, z_s.at[d], z_r.at[d, dist - 1], zdev(d, dist))
 
     def z_sent(d):
         ref = gz.at[pl.ds(0, half - d)]
-        return remote(ref, ref, z_s.at[d], z_r.at[d, 0], zdev(d))
+        return remote(ref, ref, z_s.at[d], z_r.at[d, 0], zdev(d, 1))
+
+    def z_step(st):
+        for came, goes in plan[st]:
+            for d in range(2):
+                if came is not None and came <= half - d:
+                    z_copy(d, came).wait_recv()
+                if goes is not None and goes <= half - d:
+                    z_copy(d, goes).start()
 
     def gx_copy(r):
         return remote(bufG.at[g, i], bufG.at[g, i], xs.at[3], xr.at[3], peer("inner", r))
@@ -288,51 +329,57 @@
             rest = rest - top.astype(f32)
         out_r[...] = acc
 
-    def rs_copy(d, st, c):
+    def rs_copy(d, way, c):
+        cut = (d, way - 1, rows_of(c), lanes_of(c))
         return remote(
-            rs_src.at[d, st, rows_of(c), lanes_of(c)], rs_dst.at[d, st, rows_of(c), lanes_of(c)],
-            rs_s.at[d, c], rs_r.at[d, st, c], zdev(d),
+            rs_src.at[cut], rs_dst.at[cut], rs_s.at[d, c], rs_r.at[d, way - 1, c], zdev(d, way)
         )
 
     def rs_sent(d, c):
         cut = (d, pl.ds(0, half if c // 2 == d else half - 1), rows_of(c), lanes_of(c))
-        return remote(rs_src.at[cut], rs_dst.at[cut], rs_s.at[d, c], rs_r.at[d, 0, c], zdev(d))
-
-    def rs_has(d, st, c):
-        return st > 0 or c // 2 == d
+        return remote(rs_src.at[cut], rs_dst.at[cut], rs_s.at[d, c], rs_r.at[d, 0, c], zdev(d, 1))
+
+    def rs_has(d, way, c):
+        return way < half or c // 2 == d
 
     def cut_of(value, c):
         return value[(c // 2) * CR : (c // 2 + 1) * CR, (c % 2) * S : (c % 2 + 1) * S]
 
-    for st in range(half):
-        ahead = [part(behind(1 - d, half - st)) for d in range(2)] if st else [part(behind(0, half))] * 2
-        for d in range(2):
-            if st > 0:
-                z_copy(d, st - 1).wait_recv()
-            if st < half - d:
-                z_copy(d, st).start()
+    def rs_step(way):
+        ahead = [part(behind(1 - d, way)) for d in range(2)] if way < half else [part(behind(0, half))] * 2
         for cc in range(4):
             for d in range(2):
                 c = cc if d == 0 else (cc + 2) % 4
-                if not rs_has(d, st, c):
+                if not rs_has(d, way, c):
                     continue
                 acc = cut_of(ahead[d], c)
-                if st > 0 and rs_has(d, st - 1, c):
-                    rs_copy(d, st - 1, c).wait_recv()
-                    acc = acc + rs_dst[d, st - 1, rows_of(c), lanes_of(c)].astype(f32)
-                rs_src[d, st, rows_of(c), lanes_of(c)] = acc.astype(bf16)
-                rs_copy(d, st, c).start()
+                if way < half and way + 1 != JUMP and rs_has(d, way + 1, c):
+                    rs_copy(d, way + 1, c).wait_recv()
+                    acc = acc + rs_dst[d, way, rows_of(c), lanes_of(c)].astype(f32)
+                rs_src[d, way - 1, rows_of(c), lanes_of(c)] = acc.astype(bf16)
+                rs_copy(d, way, c).start()
+
+    last = max(JUMP, 1)
+    for st, way in enumerate(range(half, last - 1, -1)):
+        rs_step(way)
+        z_step(st)
+        if st == 0:
+            x_all(2).wait_recv()
+            mix_tokens()
+        if 1 <= st < JUMP:
+            rs_step(JUMP - st)
 
     mine = part(n)
-    z_copy(0, half - 1).wait_recv()
+    z_step(len(plan) - 1)
     bufG[g, i] = jnp.sum(gz[...], axis=0)
     each(NI, lambda r: gx_copy(r).start())
     for c in range(4):
         acc = cut_of(mine, c)
         for d in range(2):
-            if rs_has(d, half - 1, c):
-                rs_copy(d, half - 1, c).wait_recv()
-                acc = acc + rs_dst[d, half - 1, rows_of(c), lanes_of(c)].astype(f32)
+            for way in sorted({1, last}):
+                if rs_has(d, way, c):
+                    rs_copy(d, way, c).wait_recv()
+                    acc = acc + rs_dst[d, way - 1, rows_of(c), lanes_of(c)].astype(f32)
         finv[rows_of(c), lanes_of(c)] = acc.astype(bf16)
     if FP > FS:
         finv[FS:FP, :] = jnp.zeros((FP - FS, 2 * S), bf16)
@@ -409,19 +456,6 @@
     FS = D // NZ
     FP = -(-(FS + K) // 128) * 128
     half = NZ // 2
-    n = lax.axis_index("dp")
-
-    matches = (expert_ids[:, :, None] == jnp.arange(E, dtype=jnp.int32)).astype(jnp.int32)
-    per_token = jnp.sum(matches, axis=1)
-    earlier = jnp.cumsum(per_token, axis=0) - per_token
-    position = jnp.sum(matches * earlier[:, None, :], axis=2)
-    codes = (expert_ids + E * position).astype(bf16)
-    code_rows = (per_token * (1 + earlier)).astype(bf16)
-    grad_cols = lax.dynamic_slice_in_dim(out_grads, n * FS, FS, 1)
-    tok_cols = lax.dynamic_slice_in_dim(token_inputs, n * FS, FS, 1)
-    pay1 = jnp.concatenate((grad_cols, codes, jnp.zeros((tokens, FP - FS - K), bf16)), axis=1)
-    pay2 = jnp.concatenate((tok_cols, jnp.zeros((tokens, FP - FS), bf16), code_rows), axis=1)
-
     vmem = pl.BlockSpec(memory_space=pltpu.VMEM)
     hbm = pl.BlockSpec(memory_space=pl.ANY)
     V = pltpu.VMEM
@@ -455,7 +489,7 @@
         ),
         name="expert_backward",
     )(
-        pay1, pay2, token_inputs, router_weight,
+        expert_ids.T, out_grads, token_inputs, router_weight,
         jnp.swapaxes(gate_weight, 1, 2), jnp.swapaxes(up_weight, 1, 2), down_weight,
         jnp.swapaxes(saved_gate, 1, 2), jnp.swapaxes(saved_up, 1, 2),
     )

time: 118 us -> 112 us (0.949)
  Pallas kernels: 110 us -> 108 us
  other arithmetic: 1.84 us -> 0 us
  local copies, waits for them, and re-layouts: 4.58 us -> 2.85 us
    pallas_call x1, Pallas kernels: 110 us -> 108 us  [local(): pl.pallas_call(functools.partial(kernel, NZ, NG, NI, K), out_shape=(jax.S...]
    concatenate x2 -> x0, other arithmetic: 1.28 us -> none  [the longest x1 0.68 us: local(): jnp.concatenate((grad_cols, codes, jnp.zeros((tokens, FP - FS - K), bf16)...]
    unnamed x3 -> x2, local copies, waits for them, and re-layouts: 3.6 us -> 2.85 us
where the time goes in v3:
time: 112 us
  Pallas kernels  108 us (96%)
  local copies, waits for them, and re-layouts  2.85 us (3%)
    pallas_call x1, Pallas kernels, local(): pl.pallas_call(functools.partial(kernel, NZ, NG, NI, K), out_shape=(jax.S...  108 us
    unnamed x2, local copies, waits for them, and re-layouts  2.85 us

profile of v3, /device:TPU:1, one launch (start us, length us, event | category | flops | bytes accessed | tf_op | source)
XLA Modules:
  0.0 111.8 jit_solution(17086674160899414190)
XLA Ops:
  0.6 108.3 %expert_backward.1 = (bf16[16,224]{1,0:T(8,128)(2,1)}, f32[224,128]{1,0:T(8,128)}) custom-call(s32[8,16]{1,0:T(8,128)} %bitcast.9, bf16[16,3584]{1,0:T(8,128)(2,1)} %grads.1, bf16[16,3584]{1,0:T(8,128)(2,1)} %tok.1, f32[3584,128]{1,0:T(8,128)} %rw_hbm.1, bf16[2,64,3584]{2,1,0:T(8,128)(2,1)} %bitcast.5, bf16[2,64,3584]{2,1,0:T(8,128)(2,1)} %bitcast.6, ...), custom_call_target="tpu_custom_call" | custom-call | tf_op jit(solution)/shard_map/expert_backward/pallas_call | solution.py:478
  108.9 1.3 %copy.13 = bf16[16,224]{1,0:T(8,128)(2,1)} copy(bf16[16,224]{1,0:T(8,128)(2,1)} %get-tuple-element.4) | data formatting | bytes 14336
  110.2 1.6 %copy.14 = f32[224,128]{1,0:T(8,128)} copy(f32[224,128]{1,0:T(8,128)} %get-tuple-element.5) | data formatting | bytes 229376

commit v4 on v3

--- a/solution.py
+++ b/solution.py
@@ -60,11 +60,8 @@
     ]
 
     def each(count, fn):
-        def body(r, carry):
+        for r in sorted(range(1, count), key=lambda r: -min(r, count - r)):
             fn(r)
-            return carry
-
-        lax.fori_loop(1, count, body, 0)
 
     def peer(axis, r):
         me, size = {"group": (g, NG), "inner": (i, NI), "dp": (n, NZ)}[axis]

time: 112 us -> 111 us (level)
  no operation moved by 1% of the time
where the time goes in v4:
time: 111 us
  Pallas kernels  107 us (96%)
  local copies, waits for them, and re-layouts  2.85 us (3%)
    pallas_call x1, Pallas kernels, local(): pl.pallas_call(functools.partial(kernel, NZ, NG, NI, K), out_shape=(jax.S...  107 us
    unnamed x2, local copies, waits for them, and re-layouts  2.85 us

profile of v4, /device:TPU:1, one launch (start us, length us, event | category | flops | bytes accessed | tf_op | source)
XLA Modules:
  0.0 110.9 jit_solution(6629076421785456982)
XLA Ops:
  0.6 107.4 %expert_backward.1 = (bf16[16,224]{1,0:T(8,128)(2,1)}, f32[224,128]{1,0:T(8,128)}) custom-call(s32[8,16]{1,0:T(8,128)} %bitcast.9, bf16[16,3584]{1,0:T(8,128)(2,1)} %grads.1, bf16[16,3584]{1,0:T(8,128)(2,1)} %tok.1, f32[3584,128]{1,0:T(8,128)} %rw_hbm.1, bf16[2,64,3584]{2,1,0:T(8,128)(2,1)} %bitcast.5, bf16[2,64,3584]{2,1,0:T(8,128)(2,1)} %bitcast.6, ...), custom_call_target="tpu_custom_call" | custom-call | tf_op jit(solution)/shard_map/expert_backward/pallas_call | solution.py:475
  108.0 1.3 %copy.13 = bf16[16,224]{1,0:T(8,128)(2,1)} copy(bf16[16,224]{1,0:T(8,128)(2,1)} %get-tuple-element.4) | data formatting | bytes 14336
  109.3 1.6 %copy.14 = f32[224,128]{1,0:T(8,128)} copy(f32[224,128]{1,0:T(8,128)} %get-tuple-element.5) | data formatting | bytes 229376
